TPU v7x, 32 devices: a whole 2x2x4 slice. The times are simulated.
32 devices in a mesh: space: 16 (over z, y, x), slab: 2 (over core).
Axes of the slice: x: 2, y: 2, z: 4, core: 2. Of those that a mesh axis runs over, the one named last changes fastest.
Arguments:
- phases: float32 [8, 192, 24, 384], P(None, 'space', 'slab'), may hold values from 0 to 1
- mobility: float32 [8], replicated, may hold values from 0.02 to 0.08
- active: int32 [16, 2, 32, 8], P('space', 'slab'), may hold values from 0 to 1, as said below
- variants: float32 [8, 3], replicated, may hold values from -4 to 4
Outputs:
- evolved: float32 [8, 192, 24, 384], P(None, 'space', 'slab')
- displacement: float32 [3, 384, 24, 192], P(None, 'space', 'slab')
Inputs may be any that keep to these rules, and one draw needn't show every extreme that they name: 1 marks an order parameter that evolves in that brick; the share of active ones differs strongly between brick indices along the first dimension.
All inputs are finite; a program needn't handle non-finite values.
Results may differ from a plain program's by a relative error of at most 0.00016.
Values sent between devices are 32-bit elements; how exact they have to be, the bound alone decides.
A program may use at most 128 MiB of HBM per device.

v0:
```python
import jax
import jax.numpy as jnp
from jax import lax
from jax.sharding import PartitionSpec as P

STEPS = 3
ITERS = 4


PAIR_ENERGY = 1.5
DIAGONAL_SHIFT = 3.0
SPECTRUM_CENTRE = 12.0
SPECTRUM_RADIUS = 9.0


def padded_2(cells, sides, width):
    for axis, dim in sides:
        count = lax.axis_size(axis)
        ends = count - 1
        head = lax.slice_in_dim(cells, 0, width, axis=dim)
        tail = lax.slice_in_dim(cells, cells.shape[dim] - width, cells.shape[dim], axis=dim)
        cells = jnp.concatenate(
            [
                lax.ppermute(tail, axis, [(i, (i + 1) % count) for i in range(ends)]),
                cells,
                lax.ppermute(head, axis, [((i + 1) % count, i) for i in range(ends)]),
            ],
            axis=dim,
        )
    return cells


def relax(fields, padded, speeds):
    summed = (
        padded[:, 2:, 1:-1, 1:-1]
        + padded[:, :-2, 1:-1, 1:-1]
        + padded[:, 1:-1, 2:, 1:-1]
        + padded[:, 1:-1, :-2, 1:-1]
        + padded[:, 1:-1, 1:-1, 2:]
        + padded[:, 1:-1, 1:-1, :-2]
    )
    laplace = summed - 6.0 * fields
    squares = jnp.sum(fields * fields, axis=0)
    driving = (
        fields * fields * fields
        - fields
        + 2.0 * PAIR_ENERGY * fields * (squares - fields * fields)
        - laplace
    )
    return fields - speeds * driving


def coefficients(fields, variants):
    squared = fields * fields
    summed = jnp.sum(squared, axis=0)
    saturation = summed / (1.0 + summed)
    excess = 0.5 * saturation
    lame_first = 1.5 + saturation
    strain = jnp.einsum("pabc,pk->kabc", squared, variants, precision=lax.Precision.HIGHEST)
    dilation = strain[0] + strain[1] + strain[2]
    stress = lame_first * dilation + 2.0 * (1.0 + excess) * strain
    return jnp.concatenate([excess[None], stress], axis=0)


def shifted(padded, along, offset):
    slicer = [slice(None)] * padded.ndim
    for dimension in range(padded.ndim - 3, padded.ndim):
        lowest = 1 + (offset if dimension == padded.ndim + along else 0)
        slicer[dimension] = slice(lowest, padded.shape[dimension] - 2 + lowest)
    return padded[tuple(slicer)]


def stiffness(padded, excess_pad):
    centre = shifted(padded, -1, 0)
    excess = shifted(excess_pad, -1, 0)
    summed = DIAGONAL_SHIFT * centre
    for along in (-3, -2, -1):
        for offset in (-1, 1):
            weight = 1.0 + 0.5 * (excess + shifted(excess_pad, along, offset))
            summed = summed + weight * (centre - shifted(padded, along, offset))
    return summed


def chebyshev(forcing, operate):
    ratio_now = SPECTRUM_RADIUS / SPECTRUM_CENTRE
    residual = forcing
    direction = forcing / SPECTRUM_CENTRE
    solution = jnp.zeros_like(forcing)
    for counter in range(ITERS):
        solution = solution + direction
        residual = residual - operate(direction)
        ratio_next = 1.0 / (2.0 * SPECTRUM_CENTRE / SPECTRUM_RADIUS - ratio_now)
        direction = (
            ratio_next * ratio_now * direction + 2.0 * ratio_next / SPECTRUM_RADIUS * residual
        )
        ratio_now = ratio_next
    return solution + direction


def pad_last(padded):
    return jnp.pad(padded, ((0, 0), (0, 0), (0, 0), (1, 1)))


def derive_forcing(padded, directions):
    return jnp.stack(
        [
            0.5
            * (shifted(padded[1 + component], along, 1) - shifted(padded[1 + component], along, -1))
            for component, along in enumerate(directions)
        ]
    )


def shards(phases, mobility, active, variants):
    brick_size = phases.shape[1]
    flags = jnp.transpose(active[0].astype(jnp.float32), (2, 0, 1))
    flags = jnp.repeat(jnp.repeat(flags, brick_size, axis=1), brick_size, axis=2)
    speeds = mobility[:, None, None, None] * flags[:, None]
    fields = phases
    for counter in range(STEPS):
        padded = padded_2(fields, (("space", 1), ("slab", 2)), 1)
        fields = relax(fields, pad_last(padded), speeds)
    local = coefficients(fields, variants)
    padded = pad_last(padded_2(local, (("space", 1), ("slab", 2)), 1))
    excess_pad = padded[0]
    forcing = derive_forcing(padded, (-3, -2, -1))

    def operate_local(direction):
        widened = padded_2(direction, (("space", 1), ("slab", 2)), 1)
        return stiffness(pad_last(widened), excess_pad)

    solved = chebyshev(forcing, operate_local)
    arrived = lax.all_to_all(solved, "space", split_axis=3, concat_axis=1, tiled=True)
    return (fields, jnp.transpose(arrived, (0, 3, 2, 1)))


def solution(mesh):
    placed = (P(None, "space", "slab", None), P(), P("space", "slab", None, None), P())
    return jax.shard_map(
        shards,
        mesh=mesh,
        in_specs=placed,
        out_specs=(P(None, "space", "slab", None), P(None, "space", "slab", None)),
        check_vma=False,
    )
```

profile of v0, /device:TPU:14, one launch (start us, length us, event | category | flops | bytes accessed | tf_op | source)
XLA Modules:
  0.0 262.5 jit_solution(16091048578428653699)
XLA Ops:
  4.1 5.2 %collective-permute-start.1 = (f32[8,1,12,384]{3,0,2,1:T(8,128)S(1)}, f32[8,1,12,384]{3,0,2,1:T(8,128)S(1)}, u32[]{:S(2)}, u32[]{:S(2)}) collective-permute-start(f32[8,1,12,384]{3,0,2,1:T(8,128)S(1)} %get-tuple-element.21), channel_id=1, source_target_pairs={{0,2},{2,4},{4,6},{6,8},{8,10},{10,12},{12,14},{14,16},{16,18},{18... | collective-permute-start | bytes 442376 | tf_op jit(solution)/shard_map/ppermute | solution.py:24
  19.5 14.4 %fusion.11 = f32[8,12,12,384]{3,0,2,1:T(8,128)S(1)} fusion(f32[8,12,12,384]{3,0,2,1:T(8,128)S(1)} %copy-done.2, f32[8,14,14,386]{3,0,2,1:T(8,128)S(1)} %select_maximum_fusion.8, f32[8,14,12,384]{3,0,2,1:T(8,128)S(1)} %constant_dynamic-update-slice_fusion, f32[8,14,1,384]{3,0,2,1:T(8,128)S(1)} %collective-permute-done.3, ...), kind=kOutput, calls=%fused_computation.36 | output fusion | flops 9787399 | bytes 11698176 | tf_op jit(solution)/shard_map/sub | solution.py:47
  33.9 6.1 %collective-permute-start.5 = (f32[8,1,12,384]{3,0,2,1:T(8,128)S(1)}, f32[8,1,12,384]{3,0,2,1:T(8,128)S(1)}, u32[]{:S(2)}, u32[]{:S(2)}) collective-permute-start(f32[8,1,12,384]{3,0,2,1:T(8,128)S(1)} %get-tuple-element.18), channel_id=1, source_target_pairs={{0,2},{2,4},{4,6},{6,8},{8,10},{10,12},{12,14},{14,16},{16,18},{18... | collective-permute-start | bytes 442376 | tf_op jit(solution)/shard_map/ppermute | solution.py:24
  43.4 5.9 %collective-permute-done.4 = f32[8,1,12,384]{3,0,2,1:T(8,128)S(1)} collective-permute-done((f32[8,1,12,384]{3,0,2,1:T(8,128)S(1)}, f32[8,1,12,384]{3,0,2,1:T(8,128)S(1)}, u32[]{:S(2)}, u32[]{:S(2)}) %collective-permute-start.4) | collective-permute-done | bytes 147488 | tf_op jit(solution)/shard_map/ppermute | solution.py:26
  54.8 15.6 %fusion.16 = f32[8,12,12,384]{3,0,2,1:T(8,128)S(1)} fusion(f32[8,12,12,384]{3,0,2,1:T(8,128)S(1)} %fusion.11, f32[8,14,14,386]{3,0,2,1:T(8,128)S(1)} %select_maximum_fusion.4, f32[8,14,1,384]{3,0,2,1:T(8,128)S(1)} %collective-permute-done.7, f32[8,1,12,384]{3,0,2,1:T(8,128)S(1)} %collective-permute-done.4, ...), kind=kOutput, calls=%fused_computation.41 | output fusion | flops 11556871 | bytes 9633792 | tf_op jit(solution)/shard_map/sub | solution.py:47
  72.4 3.9 %collective-permute-start.8 = (f32[8,1,12,384]{3,0,2,1:T(8,128)S(1)}, f32[8,1,12,384]{3,0,2,1:T(8,128)S(1)}, u32[]{:S(2)}, u32[]{:S(2)}) collective-permute-start(f32[8,1,12,384]{3,0,2,1:T(8,128)S(1)} %get-tuple-element.17), channel_id=1, source_target_pairs={{2,0},{4,2},{6,4},{8,6},{10,8},{12,10},{14,12},{16,14},{18,16},{20... | collective-permute-start | bytes 442376 | tf_op jit(solution)/shard_map/ppermute | solution.py:26
  78.5 3.4 %collective-permute-done.8 = f32[8,1,12,384]{3,0,2,1:T(8,128)S(1)} collective-permute-done((f32[8,1,12,384]{3,0,2,1:T(8,128)S(1)}, f32[8,1,12,384]{3,0,2,1:T(8,128)S(1)}, u32[]{:S(2)}, u32[]{:S(2)}) %collective-permute-start.8) | collective-permute-done | bytes 147488 | tf_op jit(solution)/shard_map/ppermute | solution.py:26
  87.5 16.9 %multiply_reduce_fusion.3 = (f32[12,12,384]{2,1,0:T(8,128)S(1)}, f32[8,12,12,384]{3,0,2,1:T(8,128)S(1)}) fusion(f32[8,12,12,384]{3,0,2,1:T(8,128)S(1)} %fusion.16, f32[8,14,14,386]{3,0,2,1:T(8,128)S(1)} %select_maximum_fusion, f32[8,1,12,384]{3,0,2,1:T(8,128)S(1)} %collective-permute-done.8, f32[8,1,12,384]{3,0,2,1:T(8,128)S(1)} %collective-permute-done.9, ...), kind=kOutput, calls=%fused_computation.87 | output fusion | flops 12386311 | bytes 9854976 | tf_op jit(solution)/shard_map/sub | solution.py:47
  107.4 3.5 %collective-permute-start.12 = (f32[4,1,12,384]{3,0,2,1:T(4,128)S(1)}, f32[4,1,12,384]{3,0,2,1:T(4,128)S(1)}, u32[]{:S(2)}, u32[]{:S(2)}) collective-permute-start(f32[4,1,12,384]{3,0,2,1:T(4,128)S(1)} %get-tuple-element.28), channel_id=1, source_target_pairs={{0,2},{2,4},{4,6},{6,8},{8,10},{10,12},{12,14},{14,16},{16,18},{18... | collective-permute-start | bytes 221192 | tf_op jit(solution)/shard_map/ppermute | solution.py:24
  113.7 5.3 %collective-permute-done.13 = f32[4,1,12,384]{3,0,2,1:T(4,128)S(1)} collective-permute-done((f32[4,1,12,384]{3,0,2,1:T(4,128)S(1)}, f32[4,1,12,384]{3,0,2,1:T(4,128)S(1)}, u32[]{:S(2)}, u32[]{:S(2)}) %collective-permute-start.13) | collective-permute-done | bytes 73760 | tf_op jit(solution)/shard_map/ppermute | solution.py:26
  130.7 3.9 %collective-permute-start.17 = (f32[3,1,12,384]{3,2,1,0:T(8,128)S(1)}, f32[3,1,12,384]{3,2,1,0:T(8,128)S(1)}, u32[]{:S(2)}, u32[]{:S(2)}) collective-permute-start(f32[3,1,12,384]{3,2,1,0:T(8,128)S(1)} %get-tuple-element.45), channel_id=1, source_target_pairs={{2,0},{4,2},{6,4},{8,6},{10,8},{12,10},{14,12},{16,14},{18,16},{20... | collective-permute-start | bytes 165896 | tf_op jit(solution)/shard_map/ppermute | solution.py:26
  135.0 3.7 %collective-permute-done.17 = f32[3,1,12,384]{3,2,1,0:T(8,128)S(1)} collective-permute-done((f32[3,1,12,384]{3,2,1,0:T(8,128)S(1)}, f32[3,1,12,384]{3,2,1,0:T(8,128)S(1)}, u32[]{:S(2)}, u32[]{:S(2)}) %collective-permute-start.17) | collective-permute-done | bytes 55328 | tf_op jit(solution)/shard_map/ppermute | solution.py:26
  148.4 3.9 %collective-permute-start.21 = (f32[3,1,12,384]{3,2,1,0:T(8,128)S(1)}, f32[3,1,12,384]{3,2,1,0:T(8,128)S(1)}, u32[]{:S(2)}, u32[]{:S(2)}) collective-permute-start(f32[3,1,12,384]{3,2,1,0:T(8,128)S(1)} %get-tuple-element.43), channel_id=1, source_target_pairs={{2,0},{4,2},{6,4},{8,6},{10,8},{12,10},{14,12},{16,14},{18,16},{20... | collective-permute-start | bytes 165896 | tf_op jit(solution)/shard_map/ppermute | solution.py:26
  152.7 3.7 %collective-permute-done.21 = f32[3,1,12,384]{3,2,1,0:T(8,128)S(1)} collective-permute-done((f32[3,1,12,384]{3,2,1,0:T(8,128)S(1)}, f32[3,1,12,384]{3,2,1,0:T(8,128)S(1)}, u32[]{:S(2)}, u32[]{:S(2)}) %collective-permute-start.21) | collective-permute-done | bytes 55328 | tf_op jit(solution)/shard_map/ppermute | solution.py:26
  165.0 3.9 %collective-permute-start.25 = (f32[3,1,12,384]{3,2,1,0:T(8,128)S(1)}, f32[3,1,12,384]{3,2,1,0:T(8,128)S(1)}, u32[]{:S(2)}, u32[]{:S(2)}) collective-permute-start(f32[3,1,12,384]{3,2,1,0:T(8,128)S(1)} %get-tuple-element.41), channel_id=1, source_target_pairs={{2,0},{4,2},{6,4},{8,6},{10,8},{12,10},{14,12},{16,14},{18,16},{20... | collective-permute-start | bytes 165896 | tf_op jit(solution)/shard_map/ppermute | solution.py:26
  169.3 3.7 %collective-permute-done.25 = f32[3,1,12,384]{3,2,1,0:T(8,128)S(1)} collective-permute-done((f32[3,1,12,384]{3,2,1,0:T(8,128)S(1)}, f32[3,1,12,384]{3,2,1,0:T(8,128)S(1)}, u32[]{:S(2)}, u32[]{:S(2)}) %collective-permute-start.25) | collective-permute-done | bytes 55328 | tf_op jit(solution)/shard_map/ppermute | solution.py:26
  182.2 3.3 %collective-permute-start.29 = (f32[3,1,12,384]{3,2,1,0:T(8,128)S(1)}, f32[3,1,12,384]{3,2,1,0:T(8,128)S(1)}, u32[]{:S(2)}, u32[]{:S(2)}) collective-permute-start(f32[3,1,12,384]{3,2,1,0:T(8,128)S(1)} %get-tuple-element.39), channel_id=1, source_target_pairs={{2,0},{4,2},{6,4},{8,6},{10,8},{12,10},{14,12},{16,14},{18,16},{20... | collective-permute-start | bytes 165896 | tf_op jit(solution)/shard_map/ppermute | solution.py:26
  185.9 4.4 %collective-permute-done.29 = f32[3,1,12,384]{3,2,1,0:T(8,128)S(1)} collective-permute-done((f32[3,1,12,384]{3,2,1,0:T(8,128)S(1)}, f32[3,1,12,384]{3,2,1,0:T(8,128)S(1)}, u32[]{:S(2)}, u32[]{:S(2)}) %collective-permute-start.29) | collective-permute-done | bytes 55328 | tf_op jit(solution)/shard_map/ppermute | solution.py:26
  198.0 5.8 %copy.29 = f32[3,12,12,384]{2,1,0,3:T(8,128)} copy(f32[3,12,12,384]{3,2,1,0:T(8,128)S(1)} %fusion.46) | data formatting | bytes 1327104 | tf_op jit(solution)/shard_map/add | solution.py:97
  203.8 7.4 %reshape.61 = f32[16,1,10368]{2,1,0:T(1,128)S(1)} reshape(f32[384,3,12,12]{3,2,1,0:T(8,128)} %bitcast.46) | data formatting | bytes 1327104
  211.1 21.5 %all_to_all.18 = f32[16,1,10368]{2,1,0:T(1,128)S(1)} all-to-all(f32[16,1,10368]{2,1,0:T(1,128)S(1)} %reshape.61), channel_id=1, replica_groups=mesh['space'=16,'slab'=2] {'space'}, dimensions={0} | all-to-all | bytes 1327104 | tf_op jit(solution)/shard_map/all_to_all | solution.py:133
  235.4 8.6 %reshape.62 = f32[384,3,12,12]{3,2,1,0:T(8,128)} reshape(f32[16,10368]{1,0:T(8,128)S(1)} %reduce) | data formatting | bytes 1327104
  244.0 12.2 %copy.30 = f32[3,12,12,16,24]{1,3,4,2,0:T(8,128)} copy(f32[3,12,12,16,24]{2,1,0,4,3:T(8,128)} %bitcast.47) | data formatting | bytes 1327104 | tf_op jit(solution)/shard_map/all_to_all | solution.py:133
  256.2 6.3 %all_to_all.16 = f32[3,192,12,24]{1,3,2,0:T(8,128)} reshape(f32[3,16,12,12,24]{2,1,4,3,0:T(8,128)} %bitcast.48) | data formatting | bytes 1327104 | tf_op jit(solution)/shard_map/all_to_all | solution.py:133
  (111 shorter events, 88.6 us)
Async XLA Ops:
  1.7 12.2 %collective-permute-start = (f32[8,1,12,384]{3,0,2,1:T(8,128)S(1)}, f32[8,1,12,384]{3,0,2,1:T(8,128)S(1)}, u32[]{:S(2)}, u32[]{:S(2)}) collective-permute-start(f32[8,1,12,384]{3,0,2,1:T(8,128)S(1)} %get-tuple-element.20), channel_id=1, source_target_pairs={{2,0},{4,2},{6,4},{8,6},{10,8},{12,10},{14,12},{16,14},{18,16},{20... | collective-permute-start | bytes 442376 | tf_op jit(solution)/shard_map/ppermute | solution.py:26
  4.1 8.1 %collective-permute-start.1 = (f32[8,1,12,384]{3,0,2,1:T(8,128)S(1)}, f32[8,1,12,384]{3,0,2,1:T(8,128)S(1)}, u32[]{:S(2)}, u32[]{:S(2)}) collective-permute-start(f32[8,1,12,384]{3,0,2,1:T(8,128)S(1)} %get-tuple-element.21), channel_id=1, source_target_pairs={{0,2},{2,4},{4,6},{6,8},{8,10},{10,12},{12,14},{14,16},{16,18},{18... | collective-permute-start | bytes 442376 | tf_op jit(solution)/shard_map/ppermute | solution.py:24
  15.3 3.3 %collective-permute-start.2 = (f32[8,14,1,384]{3,0,2,1:T(8,128)S(1)}, f32[8,14,1,384]{3,0,2,1:T(8,128)S(1)}, u32[]{:S(2)}, u32[]{:S(2)}) collective-permute-start(f32[8,14,1,384]{3,0,2,1:T(8,128)S(1)} %get-tuple-element.15), channel_id=1, source_target_pairs={{1,0},{3,2},{5,4},{7,6},{9,8},{11,10},{13,12},{15,14},{17,16},{19,... | collective-permute-start | bytes 516104 | tf_op jit(solution)/shard_map/ppermute | solution.py:26
  33.9 9.5 %collective-permute-start.5 = (f32[8,1,12,384]{3,0,2,1:T(8,128)S(1)}, f32[8,1,12,384]{3,0,2,1:T(8,128)S(1)}, u32[]{:S(2)}, u32[]{:S(2)}) collective-permute-start(f32[8,1,12,384]{3,0,2,1:T(8,128)S(1)} %get-tuple-element.18), channel_id=1, source_target_pairs={{0,2},{2,4},{4,6},{6,8},{8,10},{10,12},{12,14},{14,16},{16,18},{18... | collective-permute-start | bytes 442376 | tf_op jit(solution)/shard_map/ppermute | solution.py:24
  40.0 9.3 %collective-permute-start.4 = (f32[8,1,12,384]{3,0,2,1:T(8,128)S(1)}, f32[8,1,12,384]{3,0,2,1:T(8,128)S(1)}, u32[]{:S(2)}, u32[]{:S(2)}) collective-permute-start(f32[8,1,12,384]{3,0,2,1:T(8,128)S(1)} %get-tuple-element.19), channel_id=1, source_target_pairs={{2,0},{4,2},{6,4},{8,6},{10,8},{12,10},{14,12},{16,14},{18,16},{20... | collective-permute-start | bytes 442376 | tf_op jit(solution)/shard_map/ppermute | solution.py:26
  50.6 3.3 %collective-permute-start.6 = (f32[8,14,1,384]{3,0,2,1:T(8,128)S(1)}, f32[8,14,1,384]{3,0,2,1:T(8,128)S(1)}, u32[]{:S(2)}, u32[]{:S(2)}) collective-permute-start(f32[8,14,1,384]{3,0,2,1:T(8,128)S(1)} %get-tuple-element.13), channel_id=1, source_target_pairs={{1,0},{3,2},{5,4},{7,6},{9,8},{11,10},{13,12},{15,14},{17,16},{19,... | collective-permute-start | bytes 516104 | tf_op jit(solution)/shard_map/ppermute | solution.py:26
  70.5 8.1 %collective-permute-start.9 = (f32[8,1,12,384]{3,0,2,1:T(8,128)S(1)}, f32[8,1,12,384]{3,0,2,1:T(8,128)S(1)}, u32[]{:S(2)}, u32[]{:S(2)}) collective-permute-start(f32[8,1,12,384]{3,0,2,1:T(8,128)S(1)} %get-tuple-element.16), channel_id=1, source_target_pairs={{0,2},{2,4},{4,6},{6,8},{8,10},{10,12},{12,14},{14,16},{16,18},{18... | collective-permute-start | bytes 442376 | tf_op jit(solution)/shard_map/ppermute | solution.py:24
  72.4 9.6 %collective-permute-start.8 = (f32[8,1,12,384]{3,0,2,1:T(8,128)S(1)}, f32[8,1,12,384]{3,0,2,1:T(8,128)S(1)}, u32[]{:S(2)}, u32[]{:S(2)}) collective-permute-start(f32[8,1,12,384]{3,0,2,1:T(8,128)S(1)} %get-tuple-element.17), channel_id=1, source_target_pairs={{2,0},{4,2},{6,4},{8,6},{10,8},{12,10},{14,12},{16,14},{18,16},{20... | collective-permute-start | bytes 442376 | tf_op jit(solution)/shard_map/ppermute | solution.py:26
  83.3 3.3 %collective-permute-start.10 = (f32[8,14,1,384]{3,0,2,1:T(8,128)S(1)}, f32[8,14,1,384]{3,0,2,1:T(8,128)S(1)}, u32[]{:S(2)}, u32[]{:S(2)}) collective-permute-start(f32[8,14,1,384]{3,0,2,1:T(8,128)S(1)} %get-tuple-element.11), channel_id=1, source_target_pairs={{1,0},{3,2},{5,4},{7,6},{9,8},{11,10},{13,12},{15,14},{17,16},{19,... | collective-permute-start | bytes 516104 | tf_op jit(solution)/shard_map/ppermute | solution.py:26
  107.4 6.2 %collective-permute-start.12 = (f32[4,1,12,384]{3,0,2,1:T(4,128)S(1)}, f32[4,1,12,384]{3,0,2,1:T(4,128)S(1)}, u32[]{:S(2)}, u32[]{:S(2)}) collective-permute-start(f32[4,1,12,384]{3,0,2,1:T(4,128)S(1)} %get-tuple-element.28), channel_id=1, source_target_pairs={{0,2},{2,4},{4,6},{6,8},{8,10},{10,12},{12,14},{14,16},{16,18},{18... | collective-permute-start | bytes 221192 | tf_op jit(solution)/shard_map/ppermute | solution.py:24
  111.0 8.0 %collective-permute-start.13 = (f32[4,1,12,384]{3,0,2,1:T(4,128)S(1)}, f32[4,1,12,384]{3,0,2,1:T(4,128)S(1)}, u32[]{:S(2)}, u32[]{:S(2)}) collective-permute-start(f32[4,1,12,384]{3,0,2,1:T(4,128)S(1)} %get-tuple-element.29), channel_id=1, source_target_pairs={{2,0},{4,2},{6,4},{8,6},{10,8},{12,10},{14,12},{16,14},{18,16},{20... | collective-permute-start | bytes 221192 | tf_op jit(solution)/shard_map/ppermute | solution.py:26
  120.4 3.2 %collective-permute-start.15 = (f32[4,14,1,384]{3,0,2,1:T(4,128)S(1)}, f32[4,14,1,384]{3,0,2,1:T(4,128)S(1)}, u32[]{:S(2)}, u32[]{:S(2)}) collective-permute-start(f32[4,14,1,384]{3,0,2,1:T(4,128)S(1)} %get-tuple-element.27), channel_id=1, source_target_pairs={{1,0},{3,2},{5,4},{7,6},{9,8},{11,10},{13,12},{15,14},{17,16},{19,... | collective-permute-start | bytes 258056 | tf_op jit(solution)/shard_map/ppermute | solution.py:26
  128.7 6.2 %collective-permute-start.16 = (f32[3,1,12,384]{3,2,1,0:T(8,128)S(1)}, f32[3,1,12,384]{3,2,1,0:T(8,128)S(1)}, u32[]{:S(2)}, u32[]{:S(2)}) collective-permute-start(f32[3,1,12,384]{3,2,1,0:T(8,128)S(1)} %get-tuple-element.44), channel_id=1, source_target_pairs={{0,2},{2,4},{4,6},{6,8},{8,10},{10,12},{12,14},{14,16},{16,18},{18... | collective-permute-start | bytes 165896 | tf_op jit(solution)/shard_map/ppermute | solution.py:24
  130.7 8.0 %collective-permute-start.17 = (f32[3,1,12,384]{3,2,1,0:T(8,128)S(1)}, f32[3,1,12,384]{3,2,1,0:T(8,128)S(1)}, u32[]{:S(2)}, u32[]{:S(2)}) collective-permute-start(f32[3,1,12,384]{3,2,1,0:T(8,128)S(1)} %get-tuple-element.45), channel_id=1, source_target_pairs={{2,0},{4,2},{6,4},{8,6},{10,8},{12,10},{14,12},{16,14},{18,16},{20... | collective-permute-start | bytes 165896 | tf_op jit(solution)/shard_map/ppermute | solution.py:26
  138.8 3.3 %collective-permute-start.18 = (f32[3,14,1,384]{3,2,1,0:T(1,128)S(1)}, f32[3,14,1,384]{3,2,1,0:T(1,128)S(1)}, u32[]{:S(2)}, u32[]{:S(2)}) collective-permute-start(f32[3,14,1,384]{3,2,1,0:T(1,128)S(1)} %get-tuple-element.36), channel_id=1, source_target_pairs={{0,1},{2,3},{4,5},{6,7},{8,9},{10,11},{12,13},{14,15},{16,17},{18,... | collective-permute-start | bytes 193544 | tf_op jit(solution)/shard_map/ppermute | solution.py:24
  140.3 3.1 %collective-permute-start.19 = (f32[3,14,1,384]{3,2,1,0:T(1,128)S(1)}, f32[3,14,1,384]{3,2,1,0:T(1,128)S(1)}, u32[]{:S(2)}, u32[]{:S(2)}) collective-permute-start(f32[3,14,1,384]{3,2,1,0:T(1,128)S(1)} %get-tuple-element.37), channel_id=1, source_target_pairs={{1,0},{3,2},{5,4},{7,6},{9,8},{11,10},{13,12},{15,14},{17,16},{19,... | collective-permute-start | bytes 193544 | tf_op jit(solution)/shard_map/ppermute | solution.py:26
  146.5 6.2 %collective-permute-start.20 = (f32[3,1,12,384]{3,2,1,0:T(8,128)S(1)}, f32[3,1,12,384]{3,2,1,0:T(8,128)S(1)}, u32[]{:S(2)}, u32[]{:S(2)}) collective-permute-start(f32[3,1,12,384]{3,2,1,0:T(8,128)S(1)} %get-tuple-element.42), channel_id=1, source_target_pairs={{0,2},{2,4},{4,6},{6,8},{8,10},{10,12},{12,14},{14,16},{16,18},{18... | collective-permute-start | bytes 165896 | tf_op jit(solution)/shard_map/ppermute | solution.py:24
  148.4 8.0 %collective-permute-start.21 = (f32[3,1,12,384]{3,2,1,0:T(8,128)S(1)}, f32[3,1,12,384]{3,2,1,0:T(8,128)S(1)}, u32[]{:S(2)}, u32[]{:S(2)}) collective-permute-start(f32[3,1,12,384]{3,2,1,0:T(8,128)S(1)} %get-tuple-element.43), channel_id=1, source_target_pairs={{2,0},{4,2},{6,4},{8,6},{10,8},{12,10},{14,12},{16,14},{18,16},{20... | collective-permute-start | bytes 165896 | tf_op jit(solution)/shard_map/ppermute | solution.py:26
  157.8 3.1 %collective-permute-start.23 = (f32[3,14,1,384]{3,2,1,0:T(1,128)S(1)}, f32[3,14,1,384]{3,2,1,0:T(1,128)S(1)}, u32[]{:S(2)}, u32[]{:S(2)}) collective-permute-start(f32[3,14,1,384]{3,2,1,0:T(1,128)S(1)} %get-tuple-element.35), channel_id=1, source_target_pairs={{1,0},{3,2},{5,4},{7,6},{9,8},{11,10},{13,12},{15,14},{17,16},{19,... | collective-permute-start | bytes 193544 | tf_op jit(solution)/shard_map/ppermute | solution.py:26
  163.1 6.2 %collective-permute-start.24 = (f32[3,1,12,384]{3,2,1,0:T(8,128)S(1)}, f32[3,1,12,384]{3,2,1,0:T(8,128)S(1)}, u32[]{:S(2)}, u32[]{:S(2)}) collective-permute-start(f32[3,1,12,384]{3,2,1,0:T(8,128)S(1)} %get-tuple-element.40), channel_id=1, source_target_pairs={{0,2},{2,4},{4,6},{6,8},{8,10},{10,12},{12,14},{14,16},{16,18},{18... | collective-permute-start | bytes 165896 | tf_op jit(solution)/shard_map/ppermute | solution.py:24
  165.0 8.0 %collective-permute-start.25 = (f32[3,1,12,384]{3,2,1,0:T(8,128)S(1)}, f32[3,1,12,384]{3,2,1,0:T(8,128)S(1)}, u32[]{:S(2)}, u32[]{:S(2)}) collective-permute-start(f32[3,1,12,384]{3,2,1,0:T(8,128)S(1)} %get-tuple-element.41), channel_id=1, source_target_pairs={{2,0},{4,2},{6,4},{8,6},{10,8},{12,10},{14,12},{16,14},{18,16},{20... | collective-permute-start | bytes 165896 | tf_op jit(solution)/shard_map/ppermute | solution.py:26
  174.4 3.1 %collective-permute-start.27 = (f32[3,14,1,384]{3,2,1,0:T(1,128)S(1)}, f32[3,14,1,384]{3,2,1,0:T(1,128)S(1)}, u32[]{:S(2)}, u32[]{:S(2)}) collective-permute-start(f32[3,14,1,384]{3,2,1,0:T(1,128)S(1)} %get-tuple-element.33), channel_id=1, source_target_pairs={{1,0},{3,2},{5,4},{7,6},{9,8},{11,10},{13,12},{15,14},{17,16},{19,... | collective-permute-start | bytes 193544 | tf_op jit(solution)/shard_map/ppermute | solution.py:26
  179.7 6.2 %collective-permute-start.28 = (f32[3,1,12,384]{3,2,1,0:T(8,128)S(1)}, f32[3,1,12,384]{3,2,1,0:T(8,128)S(1)}, u32[]{:S(2)}, u32[]{:S(2)}) collective-permute-start(f32[3,1,12,384]{3,2,1,0:T(8,128)S(1)} %get-tuple-element.38), channel_id=1, source_target_pairs={{0,2},{2,4},{4,6},{6,8},{8,10},{10,12},{12,14},{14,16},{16,18},{18... | collective-permute-start | bytes 165896 | tf_op jit(solution)/shard_map/ppermute | solution.py:24
  182.2 8.0 %collective-permute-start.29 = (f32[3,1,12,384]{3,2,1,0:T(8,128)S(1)}, f32[3,1,12,384]{3,2,1,0:T(8,128)S(1)}, u32[]{:S(2)}, u32[]{:S(2)}) collective-permute-start(f32[3,1,12,384]{3,2,1,0:T(8,128)S(1)} %get-tuple-element.39), channel_id=1, source_target_pairs={{2,0},{4,2},{6,4},{8,6},{10,8},{12,10},{14,12},{16,14},{18,16},{20... | collective-permute-start | bytes 165896 | tf_op jit(solution)/shard_map/ppermute | solution.py:26
  (13 other events, 141.0 us)
where the time goes:
time: 268 us; the launch traced here: 262 us
  starting transfers between devices  71.6 us (27%)
  other arithmetic  68.3 us (25%)
  waiting for transfers between devices  52.4 us (20%)
  local copies, waits for them, and re-layouts  45.7 us (17%)
  blocking collectives  21.5 us (8%)
    sub x3, other arithmetic, relax(): squares - fields * fields  46.9 us
    ppermute x16, waiting for transfers between devices, padded_2(): lax.ppermute(head, axis, [((i + 1) % count, i) for i in range(ends)])  44.7 us
    ppermute x16, starting transfers between devices, padded_2(): lax.ppermute(head, axis, [((i + 1) % count, i) for i in range(ends)])  36 us
    ppermute x16, starting transfers between devices, padded_2(): lax.ppermute(tail, axis, [(i, (i + 1) % count) for i in range(ends)])  35.6 us
    all_to_all x1, blocking collectives, shards(): lax.all_to_all(solved, 'space', split_axis=3, concat_axis=1, tiled=True)  21.5 us
    all_to_all x3, local copies, waits for them, and re-layouts, shards(): lax.all_to_all(solved, 'space', split_axis=3, concat_axis=1, tiled=True)  19 us
    unnamed x16, local copies, waits for them, and re-layouts  17.7 us
    concatenate x10, other arithmetic, padded_2(): jnp.concatenate([lax.ppermute(tail, axis, [(i, (i + 1) % count) for i in...  9.6 us
  transfers between devices with their start and end apart: 32, of which 23 were waited for; matrix products, arithmetic and copies ran while one was open for 1% of the time, Pallas kernels for 0%

commit v1 on v0

v1 whole, which is shorter than its diff:
```python
import functools

import jax
import jax.numpy as jnp
from jax import lax
from jax.experimental import pallas as pl
from jax.experimental.pallas import tpu as pltpu
from jax.sharding import PartitionSpec as P

STEPS = 3
ITERS = 4
PAIR_ENERGY = 1.5
DIAGONAL_SHIFT = 3.0
CENTRE = 12.0
RADIUS = 9.0


def ratios():
    now = RADIUS / CENTRE
    out = []
    for _ in range(ITERS):
        later = 1.0 / (2.0 * CENTRE / RADIUS - now)
        out.append((later * now, 2.0 * later / RADIUS))
        now = later
    return out


def kernel(
    sizes,
    phases,
    speeds,
    variants,
    evolved,
    moved,
    field_a,
    field_b,
    coef,
    stress_k,
    weights,
    diagonal,
    dir_a,
    dir_b,
    residual,
    total,
    flat,
    fsi,
    fri,
    fsj,
    frj,
    csi,
    cri,
    csj,
    crj,
    dsi,
    dri,
    dsj,
    drj,
    send_sem,
    recv_sem,
):
    ns, nl, np_, ni, nj, nk, jp = sizes
    space, slab = lax.axis_index("space"), lax.axis_index("slab")
    targets = (
        (space < ns - 1, {"space": jnp.minimum(space + 1, ns - 1)}),
        (space > 0, {"space": jnp.maximum(space - 1, 0)}),
        (slab < nl - 1, {"slab": jnp.minimum(slab + 1, nl - 1)}),
        (slab > 0, {"slab": jnp.maximum(slab - 1, 0)}),
    )
    barrier = pltpu.get_barrier_semaphore()
    for has, where in targets:

        @pl.when(has)
        def _(where=where):
            pl.semaphore_signal(
                barrier, inc=1, device_id=where, device_id_type=pl.DeviceIdType.MESH
            )

    peers = jnp.minimum(space, 1) + jnp.minimum(ns - 1 - space, 1)
    peers = peers + jnp.minimum(slab, 1) + jnp.minimum(nl - 1 - slab, 1)
    pl.semaphore_wait(barrier, peers)

    def buffers(stage):
        if stage < STEPS:
            return fsi.at[stage], fri.at[stage], fsj.at[stage], frj.at[stage]
        if stage == STEPS:
            return csi, cri, csj, crj
        at = stage - STEPS - 1
        return dsi.at[at], dri.at[at], dsj.at[at], drj.at[at]

    def copy(stage, way):
        si, ri, sj, rj = buffers(stage)
        source, landing = (si, ri) if way < 2 else (sj, rj)
        return pltpu.make_async_remote_copy(
            src_ref=source.at[way % 2],
            dst_ref=landing.at[way % 2],
            send_sem=send_sem.at[stage, way],
            recv_sem=recv_sem.at[stage, way],
            device_id=targets[way][1],
            device_id_type=pl.DeviceIdType.MESH,
        )

    def send_i(stage, read):
        count, si = read(0)[0], buffers(stage)[0]
        for side in (0, 1):

            @pl.when(targets[side][0])
            def _(side=side):
                plane = ni if side == 0 else 1
                for p in range(count):
                    si[side, p * nj : (p + 1) * nj, :] = read(p)[1](plane)
                copy(stage, side).start()

    def send_j(stage, read):
        count, sj = read(0)[0], buffers(stage)[2]
        for side in (0, 1):

            @pl.when(targets[2 + side][0])
            def _(side=side):
                row = nj - 1 if side == 0 else 0

                def body(i, _):
                    for p in range(count):
                        sj[side, i, p : p + 1, :] = read(p)[2](i + 1, row)
                    return 0

                lax.fori_loop(0, ni, body, 0)
                copy(stage, 2 + side).start()

    def take_i(stage, write):
        count, ri = write(0)[0], buffers(stage)[1]
        for side in (0, 1):

            @pl.when(targets[1 - side][0])
            def _(side=side):
                copy(stage, side).wait_recv()
                plane = 0 if side == 0 else ni + 1
                for p in range(count):
                    write(p)[1](plane, ri[side, p * nj : (p + 1) * nj, :])

    def take_j(stage, write):
        count, rj = write(0)[0], buffers(stage)[3]
        for side in (0, 1):

            @pl.when(targets[3 - side][0])
            def _(side=side):
                copy(stage, 2 + side).wait_recv()
                row = jp - 1 if side == 0 else nj

                def body(i, _):
                    for p in range(count):
                        write(p)[2](i + 1, row, rj[side, i, p : p + 1, :])
                    return 0

                lax.fori_loop(0, ni, body, 0)

    def reader(ref, count, slots_i=None, slots_j=None):
        def read(p):
            pi = slots_i[p] if slots_i else p
            pj = slots_j[p] if slots_j else p
            return (
                count,
                lambda plane: ref[plane, pi, 0:nj, :],
                lambda plane, row: ref[plane, pj, row : row + 1, :],
            )

        return read

    def writer(ref, count, slots_i=None, slots_j=None):
        def write(p):
            pi = slots_i[p] if slots_i else p
            pj = slots_j[p] if slots_j else p

            def whole(plane, value):
                ref[plane, pi, 0:nj, :] = value

            def line(plane, row, value):
                ref[plane, pj, row : row + 1, :] = value

            return count, whole, line

        return write

    def stage_in(i, _):
        for p in range(np_):
            field_a[i + 1, p, 0:nj, :] = phases[p, i]
        return 0

    lax.fori_loop(0, ni, stage_in, 0)
    send_i(0, reader(field_a, np_))
    send_j(0, reader(field_a, np_))
    for ref in (field_a, field_b, coef, dir_a, dir_b):
        count = ref.shape[1]
        blank = jnp.zeros((jp, nk), jnp.float32)
        for p in range(count):
            ref[0, p] = blank
            ref[ni + 1, p] = blank

        def clear(i, _, ref=ref, count=count):
            for p in range(count):
                ref[i + 1, p, nj:jp, :] = jnp.zeros((jp - nj, nk), jnp.float32)
            return 0

        lax.fori_loop(0, ni, clear, 0)
    flat[...] = jnp.zeros_like(flat)

    lane = lax.broadcasted_iota(jnp.int32, (jp, nk), 1)
    first, last = lane == 0, lane == nk - 1

    def up(x):
        return pltpu.roll(x, jp - 1, 0)

    def down(x):
        return pltpu.roll(x, 1, 0)

    def after(x):
        return pltpu.roll(x, nk - 1, 1)

    def before(x):
        return pltpu.roll(x, 1, 1)

    def relax(i, src, store):
        squares = None
        for p in range(np_):
            x = src[i, p]
            squares = x * x if squares is None else squares + x * x
        scaled = 2.0 * PAIR_ENERGY * squares + 5.0
        for p in range(np_):
            x = src[i, p]
            around = src[i + 1, p] + src[i - 1, p] + up(x) + down(x)
            around = around + jnp.where(last, 0.0, after(x)) + jnp.where(first, 0.0, before(x))
            driving = x * (scaled + (1.0 - 2.0 * PAIR_ENERGY) * (x * x)) - around
            store(i, p, x - speeds[p : p + 1, :] * driving)

    def run(plane, stage, write):
        take_j(stage, write)
        lax.fori_loop(2, ni, lambda i, _: (plane(i), 0)[1], 0)
        take_i(stage, write)
        plane(1)
        plane(ni)

    pair = (field_a, field_b)
    for step in range(STEPS - 1):
        src, dst = pair[step % 2], pair[(step + 1) % 2]

        def store(i, p, value, dst=dst):
            dst[i, p, 0:nj, :] = value[0:nj]

        run(lambda i, src=src, store=store: relax(i, src, store), step, writer(src, np_))
        send_i(step + 1, reader(dst, np_))
        send_j(step + 1, reader(dst, np_))

    src = pair[(STEPS - 1) % 2]

    def finish(i):
        sums = [None] * 4

        def store(i, p, value):
            evolved[p, i - 1] = value[0:nj]
            square = value * value
            terms = [square] + [square * variants[p, c] for c in range(3)]
            for at, term in enumerate(terms):
                sums[at] = term if sums[at] is None else sums[at] + term

        relax(i, src, store)
        saturation = sums[0] / (1.0 + sums[0])
        excess = 0.5 * saturation
        common = (1.5 + saturation) * (sums[1] + sums[2] + sums[3])
        twice = 2.0 * (1.0 + excess)
        coef[i, 0, 0:nj, :] = excess[0:nj]
        coef[i, 1, 0:nj, :] = (common + twice * sums[1])[0:nj]
        coef[i, 2, 0:nj, :] = (common + twice * sums[2])[0:nj]
        stress_k[i] = common + twice * sums[3]

    run(finish, STEPS - 1, writer(src, np_))
    send_i(STEPS, reader(coef, 2, (0, 1), (0, 2)))
    send_j(STEPS, reader(coef, 2, (0, 1), (0, 2)))

    def prepare(i):
        excess = coef[i, 0]
        own = 1.0 + 0.5 * excess
        around = [
            coef[i + 1, 0],
            coef[i - 1, 0],
            up(excess),
            down(excess),
            jnp.where(last, 0.0, after(excess)),
            jnp.where(first, 0.0, before(excess)),
        ]
        around = [own + 0.5 * e for e in around]
        diagonal[i] = DIAGONAL_SHIFT + (
            ((around[0] + around[1]) + (around[2] + around[3])) + (around[4] + around[5])
        )
        around[4] = jnp.where(last, 0.0, around[4])
        around[5] = jnp.where(first, 0.0, around[5])
        for at in range(6):
            weights[i, at] = around[at]
        second, third = coef[i, 2], stress_k[i]
        forcing = (
            0.5 * (coef[i + 1, 1] - coef[i - 1, 1]),
            0.5 * (up(second) - down(second)),
            0.5 * (jnp.where(last, 0.0, after(third)) - jnp.where(first, 0.0, before(third))),
        )
        for c in range(3):
            residual[i, c] = forcing[c]
            dir_a[i, c, 0:nj, :] = (forcing[c] * (1.0 / CENTRE))[0:nj]

    run(prepare, STEPS, writer(coef, 2, (0, 1), (0, 2)))
    send_i(STEPS + 1, reader(dir_a, 3))
    send_j(STEPS + 1, reader(dir_a, 3))

    pair = (dir_a, dir_b)
    for turn, (keep, gain) in enumerate(ratios()):
        src, dst = pair[turn % 2], pair[(turn + 1) % 2]

        def iterate(i, src=src, dst=dst, turn=turn, keep=keep, gain=gain):
            for c in range(3):
                v = src[i, c]
                applied = diagonal[i] * v - weights[i, 0] * src[i + 1, c]
                applied = applied - weights[i, 1] * src[i - 1, c]
                applied = applied - weights[i, 2] * up(v) - weights[i, 3] * down(v)
                applied = applied - weights[i, 4] * after(v) - weights[i, 5] * before(v)
                left = residual[i, c] - applied
                so_far = v if turn == 0 else total[i, c] + v
                fresh = keep * v + gain * left
                if turn < ITERS - 1:
                    residual[i, c] = left
                    total[i, c] = so_far
                    dst[i, c, 0:nj, :] = fresh[0:nj]
                else:
                    flat[c, i - 1] = (so_far + fresh)[0:nj]

        stage = STEPS + 1 + turn
        run(iterate, stage, writer(src, 3))
        if turn < ITERS - 1:
            send_i(stage + 1, reader(dst, 3))
            send_j(stage + 1, reader(dst, 3))

    moved[...] = flat[...]
    for stage in range(STEPS + 1 + ITERS):
        for way in range(4):

            @pl.when(targets[way][0])
            def _(stage=stage, way=way):
                copy(stage, way).wait_send()


def shards(mesh, phases, mobility, active, variants):
    np_, ni, nj, nk = phases.shape
    ns, nl = mesh.shape["space"], mesh.shape["slab"]
    jp = -(-(nj + 2) // 8) * 8
    flags = jnp.transpose(active[0, 0].astype(jnp.float32), (1, 0))
    speeds = mobility[:, None] * jnp.repeat(flags, nk // flags.shape[1], axis=1)
    vmem = pl.BlockSpec(memory_space=pltpu.VMEM)
    f32 = jnp.float32
    stages = STEPS + 1 + ITERS

    def scratch(*shape):
        return pltpu.VMEM(shape, f32)

    fields, solved = pl.pallas_call(
        functools.partial(kernel, (ns, nl, np_, ni, nj, nk, jp)),
        out_shape=(
            jax.ShapeDtypeStruct(phases.shape, f32),
            jax.ShapeDtypeStruct((3, ni, nj, nk), f32),
        ),
        in_specs=[vmem, vmem, pl.BlockSpec(memory_space=pltpu.SMEM)],
        out_specs=(vmem, vmem),
        scratch_shapes=[
            scratch(ni + 2, np_, jp, nk),
            scratch(ni + 2, np_, jp, nk),
            scratch(ni + 2, 3, jp, nk),
            scratch(ni + 2, jp, nk),
            scratch(ni + 2, 6, jp, nk),
            scratch(ni + 2, jp, nk),
            scratch(ni + 2, 3, jp, nk),
            scratch(ni + 2, 3, jp, nk),
            scratch(ni + 2, 3, jp, nk),
            scratch(ni + 2, 3, jp, nk),
            scratch(3, ni, nj, nk),
            scratch(STEPS, 2, np_ * nj, nk),
            scratch(STEPS, 2, np_ * nj, nk),
            scratch(STEPS, 2, ni, np_, nk),
            scratch(STEPS, 2, ni, np_, nk),
            scratch(2, 2 * nj, nk),
            scratch(2, 2 * nj, nk),
            scratch(2, ni, 2, nk),
            scratch(2, ni, 2, nk),
            scratch(ITERS, 2, 3 * nj, nk),
            scratch(ITERS, 2, 3 * nj, nk),
            scratch(ITERS, 2, ni, 3, nk),
            scratch(ITERS, 2, ni, 3, nk),
            pltpu.SemaphoreType.DMA((stages, 4)),
            pltpu.SemaphoreType.DMA((stages, 4)),
        ],
        compiler_params=pltpu.CompilerParams(
            collective_id=0, has_side_effects=True, vmem_limit_bytes=48 * 1024 * 1024
        ),
    )(phases, speeds, variants)
    arrived = lax.all_to_all(solved, "space", split_axis=3, concat_axis=1, tiled=True)
    return fields, jnp.transpose(arrived, (0, 3, 2, 1))


def solution(mesh):
    placed = (P(None, "space", "slab", None), P(), P("space", "slab", None, None), P())
    return jax.shard_map(
        functools.partial(shards, mesh),
        mesh=mesh,
        in_specs=placed,
        out_specs=(P(None, "space", "slab", None), P(None, "space", "slab", None)),
        check_vma=False,
    )
```

time: 268 us -> 124 us (0.46)
  the two profiles are of different devices: /device:TPU:14 before, /device:TPU:0 now
where the time goes in v1:
time: 124 us; the launch traced here: 123 us
  Pallas kernels  53.4 us (43%)
  local copies, waits for them, and re-layouts  46.3 us (37%)
  waiting for transfers between devices  13.9 us (11%)
  starting transfers between devices  5.82 us (5%)
  other arithmetic  2.98 us (2%)
    pallas_call x1, Pallas kernels, shards(): pl.pallas_call(functools.partial(kernel, (ns, nl, np_, ni, nj, nk, jp)),...  53.4 us
    unnamed x7, local copies, waits for them, and re-layouts  21.5 us
    all_to_all x3, local copies, waits for them, and re-layouts, shards(): lax.all_to_all(solved, 'space', split_axis=3, concat_axis=1, tiled=True)  18.9 us
    all_to_all x1, waiting for transfers between devices, shards(): lax.all_to_all(solved, 'space', split_axis=3, concat_axis=1, tiled=True)  13.9 us
    all_to_all x1, starting transfers between devices, shards(): lax.all_to_all(solved, 'space', split_axis=3, concat_axis=1, tiled=True)  5.82 us
    pallas_call x1, local copies, waits for them, and re-layouts, shards(): pl.pallas_call(functools.partial(kernel, (ns, nl, np_, ni, nj, nk, jp)),...  5.74 us
  transfers between devices with their start and end apart: 1, of which 1 were waited for; matrix products, arithmetic and copies ran while one was open for 2% of the time, Pallas kernels for 0%

profile of v1, /device:TPU:0, one launch (start us, length us, event | category | flops | bytes accessed | tf_op | source)
XLA Modules:
  0.0 123.1 jit_solution(17742945150916809000)
XLA Ops:
  0.6 0.0 copy-start
  0.6 0.7 convert_bitcast_fusion
  1.3 0.8 copy.15.variants
  2.1 0.1 broadcast_in_dim.4
  2.2 0.1 reshape.9
  2.3 1.9 %copy.14.phases = f32[8,12,12,384]{3,2,1,0:T(8,128)S(1)} copy(f32[8,12,12,384]{3,0,2,1:T(8,128)} %param.4) | data formatting | bytes 3538944 | tf_op args[0]
  4.2 0.0 copy-done
  4.2 0.1 broadcast_multiply_fusion.speeds
  4.3 53.4 %shard_map.59 = (f32[8,12,12,384]{3,2,1,0:T(8,128)S(1)}, f32[3,12,12,384]{3,2,1,0:T(8,128)S(1)}) custom-call(f32[8,12,12,384]{3,2,1,0:T(8,128)S(1)} %copy.14.phases, f32[8,384]{1,0:T(8,128)S(1)} %broadcast_multiply_fusion.speeds, f32[8,3]{1,0:T(8,128)S(1)} %copy.15.variants), custom_call_target="tpu_custom_call" | custom-call | tf_op jit(solution)/shard_map/pallas_call | solution.py:360
  57.7 5.7 %copy.16 = f32[3,12,12,384]{2,1,0,3:T(8,128)} copy(f32[3,12,12,384]{3,2,1,0:T(8,128)S(1)} %get-tuple-element.5) | data formatting | bytes 1327104 | tf_op jit(solution)/shard_map/pallas_call | solution.py:360
  63.4 8.1 %reshape.10 = f32[16,1,10368]{2,1,0:T(1,128)} reshape(f32[384,3,12,12]{3,2,1,0:T(8,128)} %bitcast.13) | data formatting | bytes 1327104
  71.5 5.8 %all-to-all-start = ((f32[16,1,10368]{2,1,0:T(1,128)}), f32[16,1,10368]{2,1,0:T(1,128)S(1)}, u32[]{:S(2)}, u32[]{:S(2)}) async-start(f32[16,1,10368]{2,1,0:T(1,128)} %reshape.10), calls=%async_computation | async-start | bytes 1327104 | tf_op jit(solution)/shard_map/all_to_all | solution.py:399
  77.3 2.2 %copy.18 = f32[8,12,12,384]{3,0,2,1:T(8,128)} copy(f32[8,12,12,384]{3,2,1,0:T(8,128)S(1)} %get-tuple-element.10) | data formatting | bytes 3538944
  79.5 13.9 %all-to-all-done = f32[16,1,10368]{2,1,0:T(1,128)S(1)} async-done(((f32[16,1,10368]{2,1,0:T(1,128)}), f32[16,1,10368]{2,1,0:T(1,128)S(1)}, u32[]{:S(2)}, u32[]{:S(2)}) %all-to-all-start) | async-done | bytes 663584 | tf_op jit(solution)/shard_map/all_to_all | solution.py:399
  93.4 0.5 broadcast.1
  94.0 2.2 %reduce = f32[16,10368]{1,0:T(8,128)S(1)} reduce(f32[16,1,10368]{2,1,0:T(1,128)S(1)} %all-to-all-done, f32[]{:T(128)} %broadcast.1), dimensions={1}, to_apply=%all_to_all.13.reduce_sub_computation | reduce | bytes 1327108 | tf_op jit(solution)/shard_map/all_to_all | solution.py:399
  96.2 8.5 %reshape.11 = f32[384,3,12,12]{3,2,1,0:T(8,128)} reshape(f32[16,10368]{1,0:T(8,128)S(1)} %reduce) | data formatting | bytes 1327104
  104.7 12.1 %copy.17 = f32[3,12,12,16,24]{1,3,4,2,0:T(8,128)} copy(f32[3,12,12,16,24]{2,1,0,4,3:T(8,128)} %bitcast.14) | data formatting | bytes 1327104 | tf_op jit(solution)/shard_map/all_to_all | solution.py:399
  116.8 6.3 %all_to_all.16 = f32[3,192,12,24]{1,3,2,0:T(8,128)} reshape(f32[3,16,12,12,24]{2,1,4,3,0:T(8,128)} %bitcast.15) | data formatting | bytes 1327104 | tf_op jit(solution)/shard_map/all_to_all | solution.py:399
Async XLA Ops:
  0.6 3.5 %copy-start = (f32[8]{0:T(128)S(1)}, f32[8]{0:T(128)}, u32[]{:S(2)}) copy-start(f32[8]{0:T(128)} %param.5) | copy-start | bytes 100
  71.5 22.0 %all-to-all-start = ((f32[16,1,10368]{2,1,0:T(1,128)}), f32[16,1,10368]{2,1,0:T(1,128)S(1)}, u32[]{:S(2)}, u32[]{:S(2)}) async-start(f32[16,1,10368]{2,1,0:T(1,128)} %reshape.10), calls=%async_computation | async-start | bytes 1327104 | tf_op jit(solution)/shard_map/all_to_all | solution.py:399

commit v2 on v1

--- a/solution.py
+++ b/solution.py
@@ -43,6 +43,9 @@
     residual,
     total,
     flat,
+    lines,
+    leaving,
+    arrived,
     fsi,
     fri,
     fsj,
@@ -57,6 +60,8 @@
     drj,
     send_sem,
     recv_sem,
+    out_sem,
+    in_sem,
 ):
     ns, nl, np_, ni, nj, nk, jp = sizes
     space, slab = lax.axis_index("space"), lax.axis_index("slab")
@@ -66,17 +71,22 @@
         (slab < nl - 1, {"slab": jnp.minimum(slab + 1, nl - 1)}),
         (slab > 0, {"slab": jnp.maximum(slab - 1, 0)}),
     )
+    mesh_id = pl.DeviceIdType.MESH
     barrier = pltpu.get_barrier_semaphore()
-    for has, where in targets:
+
+    def greet(o, _):
+        peer = {"space": lax.rem(space + o, ns)}
+        pl.semaphore_signal(barrier, inc=1, device_id=peer, device_id_type=mesh_id)
+        return 0
+
+    lax.fori_loop(1, ns, greet, 0)
+    for has, where in targets[2:]:
 
         @pl.when(has)
         def _(where=where):
-            pl.semaphore_signal(
-                barrier, inc=1, device_id=where, device_id_type=pl.DeviceIdType.MESH
-            )
-
-    peers = jnp.minimum(space, 1) + jnp.minimum(ns - 1 - space, 1)
-    peers = peers + jnp.minimum(slab, 1) + jnp.minimum(nl - 1 - slab, 1)
+            pl.semaphore_signal(barrier, inc=1, device_id=where, device_id_type=mesh_id)
+
+    peers = ns - 1 + jnp.minimum(slab, 1) + jnp.minimum(nl - 1 - slab, 1)
     pl.semaphore_wait(barrier, peers)
 
     def buffers(stage):
@@ -96,7 +106,7 @@
             send_sem=send_sem.at[stage, way],
             recv_sem=recv_sem.at[stage, way],
             device_id=targets[way][1],
-            device_id_type=pl.DeviceIdType.MESH,
+            device_id_type=mesh_id,
         )
 
     def send_i(stage, read):
@@ -201,7 +211,6 @@
             return 0
 
         lax.fori_loop(0, ni, clear, 0)
-    flat[...] = jnp.zeros_like(flat)
 
     lane = lax.broadcasted_iota(jnp.int32, (jp, nk), 1)
     first, last = lane == 0, lane == nk - 1
@@ -335,7 +344,42 @@
             send_i(stage + 1, reader(dst, 3))
             send_j(stage + 1, reader(dst, 3))
 
-    moved[...] = flat[...]
+    for c in range(3):
+        for j in range(nj):
+            row = (c * nj + j) * ni
+            lines[row : row + ni, :] = flat[c, :, j, :]
+    turned = jnp.transpose(lines[...])
+    depth = nk // ns
+    for d in range(ns):
+        leaving[d] = turned[d * depth : (d + 1) * depth, :]
+
+    def block(other, slot):
+        return pltpu.make_async_remote_copy(
+            src_ref=leaving.at[other],
+            dst_ref=arrived.at[slot],
+            send_sem=out_sem.at[other],
+            recv_sem=in_sem.at[slot],
+            device_id={"space": other},
+            device_id_type=mesh_id,
+        )
+
+    lax.fori_loop(1, ns, lambda o, _: (block(lax.rem(space + o, ns), space).start(), 0)[1], 0)
+    arrived[space] = leaving[space]
+
+    def landed(o, _):
+        other = lax.rem(space + o, ns)
+        block(other, other).wait_recv()
+        return 0
+
+    lax.fori_loop(1, ns, landed, 0)
+    for c in range(3):
+        for j in range(nj):
+            at = (c * nj + j) * ni
+            parts = [arrived[d, :, at : at + ni] for d in range(ns)]
+            moved[c, :, j, :] = jnp.concatenate(parts, axis=1)
+    lax.fori_loop(
+        1, ns, lambda o, _: (block(lax.rem(space + o, ns), space).wait_send(), 0)[1], 0
+    )
     for stage in range(STEPS + 1 + ITERS):
         for way in range(4):
 
@@ -357,11 +401,11 @@
     def scratch(*shape):
         return pltpu.VMEM(shape, f32)
 
-    fields, solved = pl.pallas_call(
+    return pl.pallas_call(
         functools.partial(kernel, (ns, nl, np_, ni, nj, nk, jp)),
         out_shape=(
             jax.ShapeDtypeStruct(phases.shape, f32),
-            jax.ShapeDtypeStruct((3, ni, nj, nk), f32),
+            jax.ShapeDtypeStruct((3, nk // ns, nj, ni * ns), f32),
         ),
         in_specs=[vmem, vmem, pl.BlockSpec(memory_space=pltpu.SMEM)],
         out_specs=(vmem, vmem),
@@ -377,6 +421,9 @@
             scratch(ni + 2, 3, jp, nk),
             scratch(ni + 2, 3, jp, nk),
             scratch(3, ni, nj, nk),
+            scratch(3 * ni * nj, nk),
+            scratch(ns, nk // ns, 3 * ni * nj),
+            scratch(ns, nk // ns, 3 * ni * nj),
             scratch(STEPS, 2, np_ * nj, nk),
             scratch(STEPS, 2, np_ * nj, nk),
             scratch(STEPS, 2, ni, np_, nk),
@@ -391,13 +438,13 @@
             scratch(ITERS, 2, ni, 3, nk),
             pltpu.SemaphoreType.DMA((stages, 4)),
             pltpu.SemaphoreType.DMA((stages, 4)),
+            pltpu.SemaphoreType.DMA((ns,)),
+            pltpu.SemaphoreType.DMA((ns,)),
         ],
         compiler_params=pltpu.CompilerParams(
             collective_id=0, has_side_effects=True, vmem_limit_bytes=48 * 1024 * 1024
         ),
     )(phases, speeds, variants)
-    arrived = lax.all_to_all(solved, "space", split_axis=3, concat_axis=1, tiled=True)
-    return fields, jnp.transpose(arrived, (0, 3, 2, 1))
 
 
 def solution(mesh):

time: 124 us -> 80 us (0.65)
  the two profiles are of different devices: /device:TPU:0 before, /device:TPU:14 now
where the time goes in v2:
time: 80 us; the launch traced here: 79.8 us
  Pallas kernels  71.3 us (89%)
  local copies, waits for them, and re-layouts  6.48 us (8%)
  other arithmetic  1.42 us (2%)
    pallas_call x1, Pallas kernels, shards(): pl.pallas_call(functools.partial(kernel, (ns, nl, np_, ni, nj, nk, jp)),...  71.3 us
    pallas_call x2, local copies, waits for them, and re-layouts, shards(): pl.pallas_call(functools.partial(kernel, (ns, nl, np_, ni, nj, nk, jp)),...  3.66 us
    unnamed x2, local copies, waits for them, and re-layouts  2.61 us

profile of v2, /device:TPU:14, one launch (start us, length us, event | category | flops | bytes accessed | tf_op | source)
XLA Modules:
  0.0 79.8 jit_solution(16358934346940445333)
XLA Ops:
  0.6 0.7 convert_bitcast_fusion
  1.3 0.8 copy.11.variants
  2.1 0.1 broadcast_in_dim.4
  2.2 0.1 reshape.9
  2.3 0.7 broadcast_multiply_fusion.speeds
  3.0 1.9 %copy.10.phases = f32[8,12,12,384]{3,2,1,0:T(8,128)S(1)} copy(f32[8,12,12,384]{3,0,2,1:T(8,128)} %param.4) | data formatting | bytes 3538944 | tf_op args[0]
  4.9 71.3 %shard_map.59 = (f32[8,12,12,384]{3,2,1,0:T(8,128)S(1)}, f32[3,24,12,192]{3,2,1,0:T(8,128)S(1)}) custom-call(f32[8,12,12,384]{3,2,1,0:T(8,128)S(1)} %copy.10.phases, f32[8,384]{1,0:T(8,128)S(1)} %broadcast_multiply_fusion.speeds, f32[8,3]{1,0:T(8,128)S(1)} %copy.11.variants), custom_call_target="tpu_custom_call" | custom-call | tf_op jit(solution)/shard_map/pallas_call | solution.py:404
  76.2 2.2 %copy.12 = f32[8,12,12,384]{3,0,2,1:T(8,128)} copy(f32[8,12,12,384]{3,2,1,0:T(8,128)S(1)} %get-tuple-element.4) | data formatting | bytes 3538944 | tf_op jit(solution)/shard_map/pallas_call | solution.py:404
  78.4 1.4 %copy.13 = f32[3,24,12,192]{3,1,2,0:T(8,128)} copy(f32[3,24,12,192]{3,2,1,0:T(8,128)S(1)} %get-tuple-element.5) | data formatting | bytes 1327104 | tf_op jit(solution)/shard_map/pallas_call | solution.py:404

commit v3 on v2

--- a/solution.py
+++ b/solution.py
@@ -28,12 +28,16 @@
 def kernel(
     sizes,
     phases,
-    speeds,
+    mobility,
+    active,
     variants,
     evolved,
     moved,
+    speeds,
     field_a,
     field_b,
+    field_c,
+    sums,
     coef,
     stress_k,
     weights,
@@ -46,10 +50,6 @@
     lines,
     leaving,
     arrived,
-    fsi,
-    fri,
-    fsj,
-    frj,
     csi,
     cri,
     csj,
@@ -90,8 +90,6 @@
     pl.semaphore_wait(barrier, peers)
 
     def buffers(stage):
-        if stage < STEPS:
-            return fsi.at[stage], fri.at[stage], fsj.at[stage], frj.at[stage]
         if stage == STEPS:
             return csi, cri, csj, crj
         at = stage - STEPS - 1
@@ -109,6 +107,31 @@
             device_id_type=mesh_id,
         )
 
+    fields = (field_a, field_b, field_c)
+
+    def face(stage, way):
+        ref, mid_i, mid_j = fields[stage], pl.ds(1, ni), pl.ds(1, nj)
+        source, landing = (
+            ((ni, mid_j), (0, mid_j)),
+            ((1, mid_j), (ni + 1, mid_j)),
+            ((mid_i, nj), (mid_i, 0)),
+            ((mid_i, 1), (mid_i, nj + 1)),
+        )[way]
+        return pltpu.make_async_remote_copy(
+            src_ref=ref.at[source],
+            dst_ref=ref.at[landing],
+            send_sem=send_sem.at[stage, way],
+            recv_sem=recv_sem.at[stage, way],
+            device_id=targets[way][1],
+            device_id_type=mesh_id,
+        )
+
+    def send_face(stage, way):
+        pl.when(targets[way][0])(lambda: face(stage, way).start())
+
+    def take_face(stage, way):
+        pl.when(targets[way ^ 1][0])(lambda: face(stage, way).wait_recv())
+
     def send_i(stage, read):
         count, si = read(0)[0], buffers(stage)[0]
         for side in (0, 1):
@@ -190,15 +213,44 @@
 
         return write
 
-    def stage_in(i, _):
-        for p in range(np_):
-            field_a[i + 1, p, 0:nj, :] = phases[p, i]
-        return 0
-
-    lax.fori_loop(0, ni, stage_in, 0)
-    send_i(0, reader(field_a, np_))
-    send_j(0, reader(field_a, np_))
-    for ref in (field_a, field_b, coef, dir_a, dir_b):
+    def stage_in(i):
+        for j in range(nj):
+            field_a[i, j + 1] = phases[i - 1, j]
+
+    stage_in(1)
+    send_face(0, 1)
+    stage_in(ni)
+    send_face(0, 0)
+    lax.fori_loop(2, ni, lambda i, _: (stage_in(i), 0)[1], 0)
+    send_face(0, 2)
+    send_face(0, 3)
+
+    def wipe(way, plane):
+        @pl.when(jnp.logical_not(targets[way][0]))
+        def _():
+            for ref in fields:
+                if way < 2:
+                    for j in range(nj):
+                        ref[plane, j + 1] = jnp.zeros((np_, nk), jnp.float32)
+                else:
+                    for i in range(ni):
+                        ref[i + 1, plane] = jnp.zeros((np_, nk), jnp.float32)
+
+    wipe(0, ni + 1)
+    wipe(1, 0)
+    wipe(2, nj + 1)
+    wipe(3, 0)
+    bricks = active.shape[0]
+    owner = lax.broadcasted_iota(jnp.int32, (bricks, nk), 1) // (nk // bricks)
+    spread = (owner == lax.broadcasted_iota(jnp.int32, (bricks, nk), 0)).astype(jnp.float32)
+    speeds[...] = lax.dot_general(
+        active[...].astype(jnp.float32) * mobility[...],
+        spread,
+        (((0,), (0,)), ((), ())),
+        precision=lax.Precision.HIGHEST,
+        preferred_element_type=jnp.float32,
+    )
+    for ref in (coef, dir_a, dir_b):
         count = ref.shape[1]
         blank = jnp.zeros((jp, nk), jnp.float32)
         for p in range(count):
@@ -227,18 +279,40 @@
     def before(x):
         return pltpu.roll(x, 1, 1)
 
-    def relax(i, src, store):
-        squares = None
-        for p in range(np_):
-            x = src[i, p]
-            squares = x * x if squares is None else squares + x * x
+    lane_8 = lax.broadcasted_iota(jnp.int32, (np_, nk), 1)
+    first_8, last_8 = lane_8 == 0, lane_8 == nk - 1
+
+    def relax(i, j, src, store):
+        x = src[i, j]
+        square = x * x
+        squares = jnp.sum(square, axis=0, keepdims=True)
         scaled = 2.0 * PAIR_ENERGY * squares + 5.0
-        for p in range(np_):
-            x = src[i, p]
-            around = src[i + 1, p] + src[i - 1, p] + up(x) + down(x)
-            around = around + jnp.where(last, 0.0, after(x)) + jnp.where(first, 0.0, before(x))
-            driving = x * (scaled + (1.0 - 2.0 * PAIR_ENERGY) * (x * x)) - around
-            store(i, p, x - speeds[p : p + 1, :] * driving)
+        around = (src[i + 1, j] + src[i - 1, j]) + (src[i, j + 1] + src[i, j - 1])
+        around = around + jnp.where(last_8, 0.0, after(x)) + jnp.where(first_8, 0.0, before(x))
+        driving = x * (scaled + (1.0 - 2.0 * PAIR_ENERGY) * square) - around
+        store(i, j, x - speeds[...] * driving)
+
+    def advance(stage, store):
+        src = fields[stage]
+
+        def rows(i, columns):
+            for j in columns:
+                relax(i, j, src, store)
+
+        lax.fori_loop(2, ni, lambda i, _: (rows(i, range(2, nj)), 0)[1], 0)
+        take_face(stage, 2)
+        take_face(stage, 3)
+        lax.fori_loop(2, ni, lambda i, _: (rows(i, (1, nj)), 0)[1], 0)
+        take_face(stage, 0)
+        rows(1, range(1, nj + 1))
+        if stage < STEPS - 1:
+            send_face(stage + 1, 1)
+        take_face(stage, 1)
+        rows(ni, range(1, nj + 1))
+        if stage < STEPS - 1:
+            send_face(stage + 1, 0)
+            send_face(stage + 1, 2)
+            send_face(stage + 1, 3)
 
     def run(plane, stage, write):
         take_j(stage, write)
@@ -247,40 +321,35 @@
         plane(1)
         plane(ni)
 
-    pair = (field_a, field_b)
     for step in range(STEPS - 1):
-        src, dst = pair[step % 2], pair[(step + 1) % 2]
-
-        def store(i, p, value, dst=dst):
-            dst[i, p, 0:nj, :] = value[0:nj]
-
-        run(lambda i, src=src, store=store: relax(i, src, store), step, writer(src, np_))
-        send_i(step + 1, reader(dst, np_))
-        send_j(step + 1, reader(dst, np_))
-
-    src = pair[(STEPS - 1) % 2]
-
-    def finish(i):
-        sums = [None] * 4
-
-        def store(i, p, value):
-            evolved[p, i - 1] = value[0:nj]
-            square = value * value
-            terms = [square] + [square * variants[p, c] for c in range(3)]
-            for at, term in enumerate(terms):
-                sums[at] = term if sums[at] is None else sums[at] + term
-
-        relax(i, src, store)
-        saturation = sums[0] / (1.0 + sums[0])
+
+        def store(i, j, value, dst=fields[step + 1]):
+            dst[i, j] = value
+
+        advance(step, store)
+
+    def finish(i, j, value):
+        evolved[i - 1, j - 1] = value
+        square = value * value
+        sums[i, 0, j - 1 : j, :] = jnp.sum(square, axis=0, keepdims=True)
+        for c in range(3):
+            scaled = square * variants[:, c : c + 1]
+            sums[i, c + 1, j - 1 : j, :] = jnp.sum(scaled, axis=0, keepdims=True)
+
+    advance(STEPS - 1, finish)
+
+    def derive(i):
+        sum_0, sum_1, sum_2, sum_3 = (sums[i, at] for at in range(4))
+        saturation = sum_0 / (1.0 + sum_0)
         excess = 0.5 * saturation
-        common = (1.5 + saturation) * (sums[1] + sums[2] + sums[3])
+        common = (1.5 + saturation) * (sum_1 + sum_2 + sum_3)
         twice = 2.0 * (1.0 + excess)
         coef[i, 0, 0:nj, :] = excess[0:nj]
-        coef[i, 1, 0:nj, :] = (common + twice * sums[1])[0:nj]
-        coef[i, 2, 0:nj, :] = (common + twice * sums[2])[0:nj]
-        stress_k[i] = common + twice * sums[3]
-
-    run(finish, STEPS - 1, writer(src, np_))
+        coef[i, 1, 0:nj, :] = (common + twice * sum_1)[0:nj]
+        coef[i, 2, 0:nj, :] = (common + twice * sum_2)[0:nj]
+        stress_k[i] = common + twice * sum_3
+
+    lax.fori_loop(1, ni + 1, lambda i, _: (derive(i), 0)[1], 0)
     send_i(STEPS, reader(coef, 2, (0, 1), (0, 2)))
     send_j(STEPS, reader(coef, 2, (0, 1), (0, 2)))
 
@@ -376,7 +445,7 @@
         for j in range(nj):
             at = (c * nj + j) * ni
             parts = [arrived[d, :, at : at + ni] for d in range(ns)]
-            moved[c, :, j, :] = jnp.concatenate(parts, axis=1)
+            moved[c, j] = jnp.concatenate(parts, axis=1)
     lax.fori_loop(
         1, ns, lambda o, _: (block(lax.rem(space + o, ns), space).wait_send(), 0)[1], 0
     )
@@ -385,15 +454,13 @@
 
             @pl.when(targets[way][0])
             def _(stage=stage, way=way):
-                copy(stage, way).wait_send()
+                (face if stage < STEPS else copy)(stage, way).wait_send()
 
 
 def shards(mesh, phases, mobility, active, variants):
     np_, ni, nj, nk = phases.shape
     ns, nl = mesh.shape["space"], mesh.shape["slab"]
     jp = -(-(nj + 2) // 8) * 8
-    flags = jnp.transpose(active[0, 0].astype(jnp.float32), (1, 0))
-    speeds = mobility[:, None] * jnp.repeat(flags, nk // flags.shape[1], axis=1)
     vmem = pl.BlockSpec(memory_space=pltpu.VMEM)
     f32 = jnp.float32
     stages = STEPS + 1 + ITERS
@@ -401,17 +468,20 @@
     def scratch(*shape):
         return pltpu.VMEM(shape, f32)
 
-    return pl.pallas_call(
+    fields, moved = pl.pallas_call(
         functools.partial(kernel, (ns, nl, np_, ni, nj, nk, jp)),
         out_shape=(
-            jax.ShapeDtypeStruct(phases.shape, f32),
-            jax.ShapeDtypeStruct((3, nk // ns, nj, ni * ns), f32),
+            jax.ShapeDtypeStruct((ni, nj, np_, nk), f32),
+            jax.ShapeDtypeStruct((3, nj, nk // ns, ni * ns), f32),
         ),
-        in_specs=[vmem, vmem, pl.BlockSpec(memory_space=pltpu.SMEM)],
+        in_specs=[vmem, vmem, vmem, vmem],
         out_specs=(vmem, vmem),
         scratch_shapes=[
-            scratch(ni + 2, np_, jp, nk),
-            scratch(ni + 2, np_, jp, nk),
+            scratch(np_, nk),
+            scratch(ni + 2, nj + 2, np_, nk),
+            scratch(ni + 2, nj + 2, np_, nk),
+            scratch(ni + 2, nj + 2, np_, nk),
+            scratch(ni + 2, 4, jp, nk),
             scratch(ni + 2, 3, jp, nk),
             scratch(ni + 2, jp, nk),
             scratch(ni + 2, 6, jp, nk),
@@ -424,10 +494,6 @@
             scratch(3 * ni * nj, nk),
             scratch(ns, nk // ns, 3 * ni * nj),
             scratch(ns, nk // ns, 3 * ni * nj),
-            scratch(STEPS, 2, np_ * nj, nk),
-            scratch(STEPS, 2, np_ * nj, nk),
-            scratch(STEPS, 2, ni, np_, nk),
-            scratch(STEPS, 2, ni, np_, nk),
             scratch(2, 2 * nj, nk),
             scratch(2, 2 * nj, nk),
             scratch(2, ni, 2, nk),
@@ -444,7 +510,8 @@
         compiler_params=pltpu.CompilerParams(
             collective_id=0, has_side_effects=True, vmem_limit_bytes=48 * 1024 * 1024
         ),
-    )(phases, speeds, variants)
+    )(jnp.transpose(phases, (1, 2, 0, 3)), mobility[None], active[0, 0], variants)
+    return jnp.transpose(fields, (2, 0, 1, 3)), jnp.transpose(moved, (0, 2, 1, 3))
 
 
 def solution(mesh):

time: 80 us -> 80.9 us (1.011)
  Pallas kernels: 71.3 us -> 74.2 us
  other arithmetic: 1.42 us -> 0 us
    pallas_call x2 -> x0, local copies, waits for them, and re-layouts: 3.66 us -> none  [shards(): pl.pallas_call(functools.partial(kernel, (ns, nl, np_, ni, nj, nk, jp)),...]
    unnamed x2 -> x8, local copies, waits for them, and re-layouts: 2.61 us -> 5.77 us
    pallas_call x1, Pallas kernels: 71.3 us -> 74.2 us  [shards(): pl.pallas_call(functools.partial(kernel, (ns, nl, np_, ni, nj, nk, jp)),...]
where the time goes in v3:
time: 80.9 us; the launch traced here: 80.7 us
  Pallas kernels  74.2 us (92%)
  local copies, waits for them, and re-layouts  5.77 us (7%)
    pallas_call x1, Pallas kernels, shards(): pl.pallas_call(functools.partial(kernel, (ns, nl, np_, ni, nj, nk, jp)),...  74.2 us
    unnamed x8, local copies, waits for them, and re-layouts  5.77 us

profile of v3, /device:TPU:14, one launch (start us, length us, event | category | flops | bytes accessed | tf_op | source)
XLA Modules:
  0.0 80.7 jit_solution(17392421381364492250)
XLA Ops:
  0.6 0.8 copy.7.variants
  1.4 0.8 copy.6
  2.1 0.0 copy-start
  2.1 1.5 %copy-done = f32[8,12,12,384]{3,0,2,1:T(8,128)S(1)} copy-done((f32[8,12,12,384]{3,0,2,1:T(8,128)S(1)}, f32[8,12,12,384]{3,0,2,1:T(8,128)}, u32[]{:S(2)}) %copy-start) | copy-done | bytes 1769496
  3.6 0.0 copy-start.1
  3.6 0.7 copy-done.1
  4.3 74.2 %shard_map.59 = (f32[12,12,8,384]{3,2,1,0:T(8,128)S(1)}, f32[3,12,24,192]{3,2,1,0:T(8,128)S(1)}) custom-call(f32[12,12,8,384]{3,2,1,0:T(8,128)S(1)} %bitcast.6, f32[1,8]{1,0:T(1,128)S(1)} %bitcast.9, s32[32,8]{1,0:T(8,128)S(1)} %bitcast.8, f32[8,3]{1,0:T(8,128)S(1)} %copy.7.variants), custom_call_target="tpu_custom_call" | custom-call | tf_op jit(solution)/shard_map/pallas_call | solution.py:471
  78.5 1.2 %copy.10 = f32[8,12,12,384]{3,0,2,1:T(8,128)} copy(f32[8,12,12,384]{3,0,2,1:T(8,128)S(1)} %bitcast.5) | data formatting | bytes 3538944
  79.7 0.9 %copy.11 = f32[3,24,12,192]{3,1,2,0:T(8,128)} copy(f32[3,24,12,192]{3,1,2,0:T(8,128)S(1)} %bitcast.7) | data formatting | bytes 1327104
Async XLA Ops:
  2.1 1.5 %copy-start = (f32[8,12,12,384]{3,0,2,1:T(8,128)S(1)}, f32[8,12,12,384]{3,0,2,1:T(8,128)}, u32[]{:S(2)}) copy-start(f32[8,12,12,384]{3,0,2,1:T(8,128)} %param.4) | copy-start | bytes 5308420
  3.6 0.7 copy-start.1

commit v4 on v2

--- a/solution.py
+++ b/solution.py
@@ -376,7 +376,7 @@
         for j in range(nj):
             at = (c * nj + j) * ni
             parts = [arrived[d, :, at : at + ni] for d in range(ns)]
-            moved[c, :, j, :] = jnp.concatenate(parts, axis=1)
+            moved[c, j] = jnp.concatenate(parts, axis=1)
     lax.fori_loop(
         1, ns, lambda o, _: (block(lax.rem(space + o, ns), space).wait_send(), 0)[1], 0
     )
@@ -401,11 +401,11 @@
     def scratch(*shape):
         return pltpu.VMEM(shape, f32)
 
-    return pl.pallas_call(
+    fields, moved = pl.pallas_call(
         functools.partial(kernel, (ns, nl, np_, ni, nj, nk, jp)),
         out_shape=(
             jax.ShapeDtypeStruct(phases.shape, f32),
-            jax.ShapeDtypeStruct((3, nk // ns, nj, ni * ns), f32),
+            jax.ShapeDtypeStruct((3, nj, nk // ns, ni * ns), f32),
         ),
         in_specs=[vmem, vmem, pl.BlockSpec(memory_space=pltpu.SMEM)],
         out_specs=(vmem, vmem),
@@ -445,6 +445,7 @@
             collective_id=0, has_side_effects=True, vmem_limit_bytes=48 * 1024 * 1024
         ),
     )(phases, speeds, variants)
+    return fields, jnp.transpose(moved, (0, 2, 1, 3))
 
 
 def solution(mesh):

time: 80 us -> 79.3 us (level)
    pallas_call x2 -> x0, local copies, waits for them, and re-layouts: 3.66 us -> none  [shards(): pl.pallas_call(functools.partial(kernel, (ns, nl, np_, ni, nj, nk, jp)),...]
    unnamed x2 -> x4, local copies, waits for them, and re-layouts: 2.61 us -> 5.75 us
where the time goes in v4:
time: 79.3 us; the launch traced here: 79.1 us
  Pallas kernels  71.1 us (90%)
  local copies, waits for them, and re-layouts  5.96 us (8%)
  other arithmetic  1.42 us (2%)
    pallas_call x1, Pallas kernels, shards(): pl.pallas_call(functools.partial(kernel, (ns, nl, np_, ni, nj, nk, jp)),...  71.1 us
    unnamed x4, local copies, waits for them, and re-layouts  5.75 us

profile of v4, /device:TPU:14, one launch (start us, length us, event | category | flops | bytes accessed | tf_op | source)
XLA Modules:
  0.0 79.1 jit_solution(10082643791519196833)
XLA Ops:
  0.6 0.7 convert_bitcast_fusion
  1.3 0.8 copy.10.variants
  2.1 0.1 broadcast_in_dim.4
  2.2 0.1 reshape.9
  2.3 0.7 broadcast_multiply_fusion.speeds
  3.0 1.9 %copy.9.phases = f32[8,12,12,384]{3,2,1,0:T(8,128)S(1)} copy(f32[8,12,12,384]{3,0,2,1:T(8,128)} %param.4) | data formatting | bytes 3538944 | tf_op args[0]
  4.9 71.1 %shard_map.59 = (f32[8,12,12,384]{3,2,1,0:T(8,128)S(1)}, f32[3,12,24,192]{3,2,1,0:T(8,128)S(1)}) custom-call(f32[8,12,12,384]{3,2,1,0:T(8,128)S(1)} %copy.9.phases, f32[8,384]{1,0:T(8,128)S(1)} %broadcast_multiply_fusion.speeds, f32[8,3]{1,0:T(8,128)S(1)} %copy.10.variants), custom_call_target="tpu_custom_call" | custom-call | tf_op jit(solution)/shard_map/pallas_call | solution.py:404
  76.0 2.2 %copy.11 = f32[8,12,12,384]{3,0,2,1:T(8,128)} copy(f32[8,12,12,384]{3,2,1,0:T(8,128)S(1)} %get-tuple-element.8) | data formatting | bytes 3538944
  78.2 0.9 %copy.13 = f32[3,24,12,192]{3,1,2,0:T(8,128)} copy(f32[3,24,12,192]{3,1,2,0:T(8,128)S(1)} %bitcast.5) | data formatting | bytes 1327104
